TPU v7x, 256 devices: a whole 4x4x8 slice. The times are simulated.
256 devices in a mesh: row: 32 (over z, x), col: 4 (over y), layer: 2 (over core).
Axes of the slice: x: 4, y: 4, z: 8, core: 2. Of those that a mesh axis runs over, the one named last changes fastest.
Arguments:
- a_blocks: bfloat16 [1024, 32, 72, 72], P('row', ('col', 'layer')), may hold values from -2.5 to 2.5
- a_columns: int32 [1024, 32], P('row', ('col', 'layer')), may hold values from 0 to 1343, as said below
- b_blocks: bfloat16 [1344, 12, 72, 72], P(('row', 'layer'), 'col'), may hold values from -0.75 to 0.75
- b_order: int32 [1344], P(('row', 'layer')), may hold values from 0 to 1343, as said below
- b_columns: int32 [1344, 12], P(('row', 'layer'), 'col'), may hold values from 0 to 167, as said below
- c_columns: int32 [1024, 40], P('row', 'col'), may hold values from 0 to 167, as said below
Outputs:
- product: bfloat16 [1024, 40, 72, 72], P(('row', 'layer'), 'col')
Inputs may be any that keep to these rules, and one draw needn't show every extreme that they name: `a_columns`: slot g of a block row names a block column l + 2 * (c * 168 + m) with c = g // 8, l = (g // 4) % 2 and 0 <= m < 168; the 4 slots of one slot group name distinct columns, and all slots of one block row have the same m % 12, the block row's region. `b_order`: A permutation of the 1344 block rows; stored row p holds a block row k with k % 2 == (p // 21) % 2. `b_columns`: each column tile is divided into 12 disjoint sets of 14 block columns, one for each region. Within one stored row and one column tile the 3 columns are distinct and lie in the set of the region (k // 2) % 12 of the stored row's block row k. `c_columns`: within one block row and one column tile the 10 columns are distinct and lie in the set of that tile and of the block row's region.
All inputs are finite; a program needn't handle non-finite values.
Results may differ from a plain program's by a relative error of at most 0.014.
Values may be sent and summed in bfloat16 or wider, within the bound.
No kernel may reach another device: no remote copies, remote signals or barrier semaphores. Data moves between devices by JAX's collectives and lax.ppermute only.
A program may use at most 256 MiB of HBM per device.

v0:
```python
import jax
import jax.numpy as jnp
from jax import lax
from jax.sharding import PartitionSpec as P

BS = 72
NB = 1344


def on_device(a_blocks, a_columns, b_blocks, b_order, b_columns, c_columns):
    rows_here = a_blocks.shape[0]
    n_cslot = c_columns.shape[1]
    panel_blocks, panel_order, panel_columns = (
        lax.all_gather(b_blocks, "row", axis=0, tiled=True),
        lax.all_gather(b_order, "row", axis=0, tiled=True),
        lax.all_gather(b_columns, "row", axis=0, tiled=True),
    )
    slab_rows = panel_order.shape[0]
    position = (
        jnp.zeros((NB,), jnp.int32).at[panel_order].set(jnp.arange(slab_rows, dtype=jnp.int32))
    )
    row_ids = jnp.arange(rows_here, dtype=jnp.int32)
    c_ids = jnp.arange(n_cslot, dtype=jnp.int32)
    initial = jnp.zeros((rows_here * n_cslot, BS, BS), jnp.float32)
    piece_blocks = lax.all_gather(a_blocks, "col", axis=1, tiled=True)
    piece_columns = lax.all_gather(a_columns, "col", axis=1, tiled=True)
    piece_width = piece_columns.shape[1]

    def one_slot(slot_number, running):
        columns_now = lax.dynamic_index_in_dim(piece_columns, slot_number, 1, keepdims=False)
        a_square = lax.dynamic_index_in_dim(piece_blocks, slot_number, 1, keepdims=False)
        stored = position[columns_now]
        b_square = panel_blocks[stored]
        products = jnp.einsum(
            "rab,rtbc->rtac", a_square, b_square, preferred_element_type=jnp.float32
        )
        matches = panel_columns[stored][:, :, None] == c_columns[:, None, :]
        found_any = jnp.any(matches, axis=2)
        slot_index = jnp.sum(jnp.where(matches, c_ids[None, None, :], 0), axis=2)
        target = jnp.where(found_any, row_ids[:, None] * n_cslot + slot_index, rows_here * n_cslot)
        return running.at[target.reshape(-1)].add(products.reshape(-1, BS, BS), mode="drop")

    accum = lax.fori_loop(0, piece_width, one_slot, initial)
    partial_sums = accum.reshape(rows_here, n_cslot, BS, BS)
    summed = lax.psum_scatter(
        partial_sums.astype(jnp.bfloat16), "layer", scatter_dimension=0, tiled=True
    )
    return summed


def solution(mesh):
    in_specs = (
        P("row", ("col", "layer"), None, None),
        P("row", ("col", "layer")),
        P(("row", "layer"), "col", None, None),
        P(("row", "layer")),
        P(("row", "layer"), "col"),
        P("row", "col"),
    )
    out_specs = P(("row", "layer"), "col", None, None)
    return jax.shard_map(
        on_device, mesh=mesh, in_specs=in_specs, out_specs=out_specs, check_vma=False
    )
```

profile of v0, /device:TPU:1, one launch (start us, length us, event | category | flops | bytes accessed | tf_op | source)
XLA Modules:
  0.0 837.3 jit_solution(3088584820271423426)
XLA Ops:
  10.8 43.8 %all-gather.1 = s32[32,21,3]{1,2,0:T(4,128)S(1)} all-gather(s32[1,21,3]{1,2,0:T(4,128)S(1)} %bitcast.47), channel_id=1, replica_groups=mesh['row'=32,'col'=4,'layer'=2] {'row'}, dimensions={0}, use_global_device_ids=true | all-gather | bytes 8316 | tf_op jit(solution)/shard_map/all_gather | solution.py:16
  56.4 14.3 %all-reduce = s32[672]{0:T(1024)S(1)} all-reduce(s32[672]{0:T(1024)S(1)} %dynamic-update-slice), channel_id=1, replica_groups=mesh['row'=32,'col'=4,'layer'=2] {'row'}, use_global_device_ids=true, to_apply=%add | all-reduce | flops 672 | bytes 5376
  74.9 9.2 %all-gather = s32[4,4,32]{2,1,0:T(4,128)S(1)} all-gather(s32[1,4,32]{2,1,0:T(4,128)S(1)} %bitcast.48), channel_id=1, replica_groups=mesh['row'=32,'col'=4,'layer'=2] {'col'}, dimensions={0}, use_global_device_ids=true | all-gather | bytes 2560 | tf_op jit(solution)/shard_map/all_gather | solution.py:26
  84.1 24.3 %all-gather.7.cloned.1.call-done = bf16[32,16,72,72]{3,2,0,1:T(8,128)(2,1)} async-done(((bf16[32,4,72,72]{3,2,0,1:T(8,128)(2,1)}), bf16[32,16,72,72]{3,2,0,1:T(8,128)(2,1)}) %all-gather.7.cloned.1.call-update) | async-done | bytes 5308432 | tf_op jit(solution)/shard_map/all_gather | solution.py:25
  108.4 257.8 %all-gather.5.cloned.1.call-done = bf16[672,3,72,72]{3,2,1,0:T(8,128)(2,1)} async-done(((bf16[21,3,72,72]{3,2,1,0:T(8,128)(2,1)}), bf16[672,3,72,72]{3,2,1,0:T(8,128)(2,1)}) %all-gather.5.cloned.1.call-update) | async-done | bytes 20901904 | tf_op jit(solution)/shard_map/all_gather | solution.py:14
  371.3 434.4 %while.14 = (s32[]{:T(128)}, f32[320,72,72]{2,1,0:T(8,128)}, s32[32,16]{0,1:T(8,128)S(1)}, s32[1344]{0:T(1024)S(1)}, s32[672,3]{1,0:T(8,128)S(1)}, /*index=5*/s3...) while((s32[]{:T(128)}, f32[320,72,72]{2,1,0:T(8,128)}, ...), condition=%wide.region_5.6_spmd.clone, body=%wide.region_1.5_spmd.clone.sunk | while | flops 72168640 | bytes 16393757 | solution.py:43
  382.5 16.0 %scatter_fusion = f32[320,72,72]{2,1,0:T(8,128)} fusion(f32[320,72,72]{2,1,0:T(8,128)} %get-tuple-element.293, s32[96]{0:T(128)} %fusion.27, f32[96,72,72]{2,1,0:T(8,128)} %copy.37), kind=kCustom, calls=%fused_computation.3.clone.clone.1 | custom fusion | flops 497664 | bytes 5972352 | tf_op jit(solution)/shard_map/while/body/eval_jaxpr/scatter-add | solution.py:41
  409.7 15.9 %scatter_fusion = f32[320,72,72]{2,1,0:T(8,128)} fusion(f32[320,72,72]{2,1,0:T(8,128)} %get-tuple-element.293, s32[96]{0:T(128)} %fusion.27, f32[96,72,72]{2,1,0:T(8,128)} %copy.37), kind=kCustom, calls=%fused_computation.3.clone.clone.1 | custom fusion | flops 497664 | bytes 5972352 | tf_op jit(solution)/shard_map/while/body/eval_jaxpr/scatter-add | solution.py:41
  436.8 16.0 %scatter_fusion = f32[320,72,72]{2,1,0:T(8,128)} fusion(f32[320,72,72]{2,1,0:T(8,128)} %get-tuple-element.293, s32[96]{0:T(128)} %fusion.27, f32[96,72,72]{2,1,0:T(8,128)} %copy.37), kind=kCustom, calls=%fused_computation.3.clone.clone.1 | custom fusion | flops 497664 | bytes 5972352 | tf_op jit(solution)/shard_map/while/body/eval_jaxpr/scatter-add | solution.py:41
  464.0 16.0 %scatter_fusion = f32[320,72,72]{2,1,0:T(8,128)} fusion(f32[320,72,72]{2,1,0:T(8,128)} %get-tuple-element.293, s32[96]{0:T(128)} %fusion.27, f32[96,72,72]{2,1,0:T(8,128)} %copy.37), kind=kCustom, calls=%fused_computation.3.clone.clone.1 | custom fusion | flops 497664 | bytes 5972352 | tf_op jit(solution)/shard_map/while/body/eval_jaxpr/scatter-add | solution.py:41
  491.1 15.9 %scatter_fusion = f32[320,72,72]{2,1,0:T(8,128)} fusion(f32[320,72,72]{2,1,0:T(8,128)} %get-tuple-element.293, s32[96]{0:T(128)} %fusion.27, f32[96,72,72]{2,1,0:T(8,128)} %copy.37), kind=kCustom, calls=%fused_computation.3.clone.clone.1 | custom fusion | flops 497664 | bytes 5972352 | tf_op jit(solution)/shard_map/while/body/eval_jaxpr/scatter-add | solution.py:41
  518.3 16.0 %scatter_fusion = f32[320,72,72]{2,1,0:T(8,128)} fusion(f32[320,72,72]{2,1,0:T(8,128)} %get-tuple-element.293, s32[96]{0:T(128)} %fusion.27, f32[96,72,72]{2,1,0:T(8,128)} %copy.37), kind=kCustom, calls=%fused_computation.3.clone.clone.1 | custom fusion | flops 497664 | bytes 5972352 | tf_op jit(solution)/shard_map/while/body/eval_jaxpr/scatter-add | solution.py:41
  545.5 16.0 %scatter_fusion = f32[320,72,72]{2,1,0:T(8,128)} fusion(f32[320,72,72]{2,1,0:T(8,128)} %get-tuple-element.293, s32[96]{0:T(128)} %fusion.27, f32[96,72,72]{2,1,0:T(8,128)} %copy.37), kind=kCustom, calls=%fused_computation.3.clone.clone.1 | custom fusion | flops 497664 | bytes 5972352 | tf_op jit(solution)/shard_map/while/body/eval_jaxpr/scatter-add | solution.py:41
  572.7 15.9 %scatter_fusion = f32[320,72,72]{2,1,0:T(8,128)} fusion(f32[320,72,72]{2,1,0:T(8,128)} %get-tuple-element.293, s32[96]{0:T(128)} %fusion.27, f32[96,72,72]{2,1,0:T(8,128)} %copy.37), kind=kCustom, calls=%fused_computation.3.clone.clone.1 | custom fusion | flops 497664 | bytes 5972352 | tf_op jit(solution)/shard_map/while/body/eval_jaxpr/scatter-add | solution.py:41
  599.9 16.0 %scatter_fusion = f32[320,72,72]{2,1,0:T(8,128)} fusion(f32[320,72,72]{2,1,0:T(8,128)} %get-tuple-element.293, s32[96]{0:T(128)} %fusion.27, f32[96,72,72]{2,1,0:T(8,128)} %copy.37), kind=kCustom, calls=%fused_computation.3.clone.clone.1 | custom fusion | flops 497664 | bytes 5972352 | tf_op jit(solution)/shard_map/while/body/eval_jaxpr/scatter-add | solution.py:41
  627.0 15.9 %scatter_fusion = f32[320,72,72]{2,1,0:T(8,128)} fusion(f32[320,72,72]{2,1,0:T(8,128)} %get-tuple-element.293, s32[96]{0:T(128)} %fusion.27, f32[96,72,72]{2,1,0:T(8,128)} %copy.37), kind=kCustom, calls=%fused_computation.3.clone.clone.1 | custom fusion | flops 497664 | bytes 5972352 | tf_op jit(solution)/shard_map/while/body/eval_jaxpr/scatter-add | solution.py:41
  654.2 15.9 %scatter_fusion = f32[320,72,72]{2,1,0:T(8,128)} fusion(f32[320,72,72]{2,1,0:T(8,128)} %get-tuple-element.293, s32[96]{0:T(128)} %fusion.27, f32[96,72,72]{2,1,0:T(8,128)} %copy.37), kind=kCustom, calls=%fused_computation.3.clone.clone.1 | custom fusion | flops 497664 | bytes 5972352 | tf_op jit(solution)/shard_map/while/body/eval_jaxpr/scatter-add | solution.py:41
  681.3 15.9 %scatter_fusion = f32[320,72,72]{2,1,0:T(8,128)} fusion(f32[320,72,72]{2,1,0:T(8,128)} %get-tuple-element.293, s32[96]{0:T(128)} %fusion.27, f32[96,72,72]{2,1,0:T(8,128)} %copy.37), kind=kCustom, calls=%fused_computation.3.clone.clone.1 | custom fusion | flops 497664 | bytes 5972352 | tf_op jit(solution)/shard_map/while/body/eval_jaxpr/scatter-add | solution.py:41
  708.4 15.9 %scatter_fusion = f32[320,72,72]{2,1,0:T(8,128)} fusion(f32[320,72,72]{2,1,0:T(8,128)} %get-tuple-element.293, s32[96]{0:T(128)} %fusion.27, f32[96,72,72]{2,1,0:T(8,128)} %copy.37), kind=kCustom, calls=%fused_computation.3.clone.clone.1 | custom fusion | flops 497664 | bytes 5972352 | tf_op jit(solution)/shard_map/while/body/eval_jaxpr/scatter-add | solution.py:41
  735.5 15.9 %scatter_fusion = f32[320,72,72]{2,1,0:T(8,128)} fusion(f32[320,72,72]{2,1,0:T(8,128)} %get-tuple-element.293, s32[96]{0:T(128)} %fusion.27, f32[96,72,72]{2,1,0:T(8,128)} %copy.37), kind=kCustom, calls=%fused_computation.3.clone.clone.1 | custom fusion | flops 497664 | bytes 5972352 | tf_op jit(solution)/shard_map/while/body/eval_jaxpr/scatter-add | solution.py:41
  762.6 16.0 %scatter_fusion = f32[320,72,72]{2,1,0:T(8,128)} fusion(f32[320,72,72]{2,1,0:T(8,128)} %get-tuple-element.293, s32[96]{0:T(128)} %fusion.27, f32[96,72,72]{2,1,0:T(8,128)} %copy.37), kind=kCustom, calls=%fused_computation.3.clone.clone.1 | custom fusion | flops 497664 | bytes 5972352 | tf_op jit(solution)/shard_map/while/body/eval_jaxpr/scatter-add | solution.py:41
  789.8 15.9 %scatter_fusion = f32[320,72,72]{2,1,0:T(8,128)} fusion(f32[320,72,72]{2,1,0:T(8,128)} %get-tuple-element.293, s32[96]{0:T(128)} %fusion.27, f32[96,72,72]{2,1,0:T(8,128)} %copy.37), kind=kCustom, calls=%fused_computation.3.clone.clone.1 | custom fusion | flops 497664 | bytes 5972352 | tf_op jit(solution)/shard_map/while/body/eval_jaxpr/scatter-add | solution.py:41
  805.8 7.6 convert_element_type.6
  813.4 17.4 %reduce-scatter.2.cloned.1.call-done = bf16[16,10,72,72]{3,2,1,0:T(8,128)(2,1)} async-done(((bf16[32,10,72,72]{3,2,1,0:T(8,128)(2,1)}), bf16[16,10,72,72]{3,2,1,0:T(8,128)(2,1)}) %reduce-scatter.2.cloned.1.call-update) | async-done | bytes 1658896 | tf_op jit(solution)/shard_map/reduce_scatter | solution.py:45
  (427 shorter events, 192.8 us)
Async XLA Ops:
  6.5 48.4 %copy-start.8 = (u32[256]{0:T(256)S(1)}, u32[256]{0:T(256)}, u32[]{:S(2)}) copy-start(u32[256]{0:T(256)} %constant.78) | copy-start | bytes 3076
  6.5 49.6 %copy-start.7 = (s32[21]{0:T(128)S(1)}, s32[21]{0:T(128)}, u32[]{:S(2)}) copy-start(s32[21]{0:T(128)} %param.11) | copy-start | bytes 256
  6.5 68.3 %copy-start.6 = (s32[32,4]{0,1:T(4,128)S(1)}, s32[32,4]{0,1:T(4,128)}, u32[]{:S(2)}) copy-start(s32[32,4]{0,1:T(4,128)} %param.9) | copy-start | bytes 1540
  6.5 101.9 %all-gather.7.cloned.1.call-start = ((), (), s32[]{:S(2)}) async-start(), calls=%async_computation.2 | async-start | bytes 11796480 | tf_op jit(solution)/shard_map/all_gather | solution.py:25
  9.9 356.3 %all-gather.5.cloned.1.call-start = ((), (), s32[]{:S(2)}) async-start(), calls=%async_computation.1 | async-start | bytes 38320128 | tf_op jit(solution)/shard_map/all_gather | solution.py:14
  10.7 820.1 %reduce-scatter.2.cloned.1.call-start = ((), (), s32[]{:S(2)}) async-start(), calls=%async_computation.3 | async-start | bytes 8847360 | tf_op jit(solution)/shard_map/reduce_scatter | solution.py:45
  382.5 16.0 %copy-start.1 = (s32[672,3]{1,0:T(8,128)S(1)}, s32[672,3]{1,0:T(8,128)}, u32[]{:S(2)}) copy-start(s32[672,3]{1,0:T(8,128)} %copy-done) | copy-start | bytes 24196 | tf_op jit(solution)/shard_map/while
  382.5 16.0 %copy-start.4 = (s32[32,16]{0,1:T(8,128)S(1)}, s32[32,16]{0,1:T(8,128)}, u32[]{:S(2)}) copy-start(s32[32,16]{0,1:T(8,128)} %copy-done.3) | copy-start | bytes 6148 | tf_op jit(solution)/shard_map/while
  436.8 16.0 %copy-start.1 = (s32[672,3]{1,0:T(8,128)S(1)}, s32[672,3]{1,0:T(8,128)}, u32[]{:S(2)}) copy-start(s32[672,3]{1,0:T(8,128)} %copy-done) | copy-start | bytes 24196 | tf_op jit(solution)/shard_map/while
  436.8 16.0 %copy-start.4 = (s32[32,16]{0,1:T(8,128)S(1)}, s32[32,16]{0,1:T(8,128)}, u32[]{:S(2)}) copy-start(s32[32,16]{0,1:T(8,128)} %copy-done.3) | copy-start | bytes 6148 | tf_op jit(solution)/shard_map/while
  464.0 16.0 %copy-start.1 = (s32[672,3]{1,0:T(8,128)S(1)}, s32[672,3]{1,0:T(8,128)}, u32[]{:S(2)}) copy-start(s32[672,3]{1,0:T(8,128)} %copy-done) | copy-start | bytes 24196 | tf_op jit(solution)/shard_map/while
  464.0 16.0 %copy-start.4 = (s32[32,16]{0,1:T(8,128)S(1)}, s32[32,16]{0,1:T(8,128)}, u32[]{:S(2)}) copy-start(s32[32,16]{0,1:T(8,128)} %copy-done.3) | copy-start | bytes 6148 | tf_op jit(solution)/shard_map/while
  491.1 15.9 %copy-start.1 = (s32[672,3]{1,0:T(8,128)S(1)}, s32[672,3]{1,0:T(8,128)}, u32[]{:S(2)}) copy-start(s32[672,3]{1,0:T(8,128)} %copy-done) | copy-start | bytes 24196 | tf_op jit(solution)/shard_map/while
  491.1 15.9 %copy-start.4 = (s32[32,16]{0,1:T(8,128)S(1)}, s32[32,16]{0,1:T(8,128)}, u32[]{:S(2)}) copy-start(s32[32,16]{0,1:T(8,128)} %copy-done.3) | copy-start | bytes 6148 | tf_op jit(solution)/shard_map/while
  518.3 16.1 %copy-start.1 = (s32[672,3]{1,0:T(8,128)S(1)}, s32[672,3]{1,0:T(8,128)}, u32[]{:S(2)}) copy-start(s32[672,3]{1,0:T(8,128)} %copy-done) | copy-start | bytes 24196 | tf_op jit(solution)/shard_map/while
  518.3 16.1 %copy-start.4 = (s32[32,16]{0,1:T(8,128)S(1)}, s32[32,16]{0,1:T(8,128)}, u32[]{:S(2)}) copy-start(s32[32,16]{0,1:T(8,128)} %copy-done.3) | copy-start | bytes 6148 | tf_op jit(solution)/shard_map/while
  545.5 16.0 %copy-start.1 = (s32[672,3]{1,0:T(8,128)S(1)}, s32[672,3]{1,0:T(8,128)}, u32[]{:S(2)}) copy-start(s32[672,3]{1,0:T(8,128)} %copy-done) | copy-start | bytes 24196 | tf_op jit(solution)/shard_map/while
  545.5 16.0 %copy-start.4 = (s32[32,16]{0,1:T(8,128)S(1)}, s32[32,16]{0,1:T(8,128)}, u32[]{:S(2)}) copy-start(s32[32,16]{0,1:T(8,128)} %copy-done.3) | copy-start | bytes 6148 | tf_op jit(solution)/shard_map/while
  599.8 16.0 %copy-start.1 = (s32[672,3]{1,0:T(8,128)S(1)}, s32[672,3]{1,0:T(8,128)}, u32[]{:S(2)}) copy-start(s32[672,3]{1,0:T(8,128)} %copy-done) | copy-start | bytes 24196 | tf_op jit(solution)/shard_map/while
  599.9 16.0 %copy-start.4 = (s32[32,16]{0,1:T(8,128)S(1)}, s32[32,16]{0,1:T(8,128)}, u32[]{:S(2)}) copy-start(s32[32,16]{0,1:T(8,128)} %copy-done.3) | copy-start | bytes 6148 | tf_op jit(solution)/shard_map/while
  627.0 15.9 %copy-start.1 = (s32[672,3]{1,0:T(8,128)S(1)}, s32[672,3]{1,0:T(8,128)}, u32[]{:S(2)}) copy-start(s32[672,3]{1,0:T(8,128)} %copy-done) | copy-start | bytes 24196 | tf_op jit(solution)/shard_map/while
  627.0 15.9 %copy-start.4 = (s32[32,16]{0,1:T(8,128)S(1)}, s32[32,16]{0,1:T(8,128)}, u32[]{:S(2)}) copy-start(s32[32,16]{0,1:T(8,128)} %copy-done.3) | copy-start | bytes 6148 | tf_op jit(solution)/shard_map/while
  762.6 16.0 %copy-start.1 = (s32[672,3]{1,0:T(8,128)S(1)}, s32[672,3]{1,0:T(8,128)}, u32[]{:S(2)}) copy-start(s32[672,3]{1,0:T(8,128)} %copy-done) | copy-start | bytes 24196 | tf_op jit(solution)/shard_map/while
  762.6 16.0 %copy-start.4 = (s32[32,16]{0,1:T(8,128)S(1)}, s32[32,16]{0,1:T(8,128)}, u32[]{:S(2)}) copy-start(s32[32,16]{0,1:T(8,128)} %copy-done.3) | copy-start | bytes 6148 | tf_op jit(solution)/shard_map/while
  (48 other events, 279.2 us)
Sparse Core Ops, SparseCore 0:
  10.1 98.3 all-gather.6
  111.0 255.1 all-gather.4
  813.5 17.2 reduce-scatter.1
where the time goes:
time: 842 us; the launch traced here: 837 us
  waiting for transfers between devices  300 us (36%)
  other arithmetic  272 us (32%)
  local copies, waits for them, and re-layouts  139 us (17%)
  blocking collectives  67.4 us (8%)
  matrix products  43.4 us (5%)
  between operations  13.8 us (2%)
    all_gather x1, waiting for transfers between devices, on_device(): lax.all_gather(b_blocks, 'row', axis=0, tiled=True)  258 us
    scatter-add x16, other arithmetic, one_slot(): running.at[target.reshape(-1)]  255 us
    gather x16, local copies, waits for them, and re-layouts, one_slot(): b_square = panel_blocks[stored]  52.8 us
    reshape x16, local copies, waits for them, and re-layouts, one_slot(): products.reshape(-1, BS, BS)  47.9 us
    all_gather x1, blocking collectives, on_device(): lax.all_gather(b_columns, 'row', axis=0, tiled=True)  43.8 us
    dot_general x16, matrix products, one_slot(): jnp.einsum('rab,rtbc->rtac', a_square, b_square, preferred_element_type=j...  43.4 us
    all_gather x1, waiting for transfers between devices, on_device(): piece_blocks = lax.all_gather(a_blocks, 'col', axis=1, tiled=True)  24.3 us
    reduce_scatter x1, waiting for transfers between devices, on_device(): lax.psum_scatter(partial_sums.astype(jnp.bfloat16), 'layer', scatter_dime...  17.4 us
  transfers between devices with their start and end apart: 3, of which 3 were waited for; matrix products, arithmetic and copies ran while one was open for 1% of the time, Pallas kernels for 0%

commit v1 on v0

v1 whole, which is shorter than its diff:
```python
import functools

import jax
import jax.numpy as jnp
from jax import lax
from jax.experimental import pallas as pl
from jax.experimental.pallas import tpu as pltpu
from jax.sharding import PartitionSpec as P

BS = 72
LANES = 128
NZB = 3
NZC = 10
KBP = 21
PAGES = 18
EXTRA = KBP - PAGES
PER = PAGES // EXTRA
PIECE = NZB * BS // PER
USED = NZB * BS
SLOTS = 16
VMEM = 48 * 1024 * 1024


def pack_b_kernel(b_ref, out_ref):
    for r in range(PAGES):
        e, j = PAGES + r // PER, r % PER
        lane = j * PIECE
        t, off = lane // BS, lane % BS
        out_ref[r] = jnp.concatenate(
            [
                b_ref[r, 0],
                b_ref[r, 1],
                b_ref[r, 2],
                b_ref[e, t][:, off : off + PIECE],
                jnp.zeros((BS, 2 * LANES - USED - PIECE), jnp.bfloat16),
            ],
            axis=1,
        )


def pack_b(b):
    return pl.pallas_call(
        pack_b_kernel,
        out_shape=jax.ShapeDtypeStruct((PAGES, BS, 2 * LANES), jnp.bfloat16),
        compiler_params=pltpu.CompilerParams(vmem_limit_bytes=VMEM),
    )(b)


def extra_kernel(p_ref, out_ref):
    lo = USED - LANES
    for e in range(EXTRA):
        pieces = [p_ref[e * PER + j][:, lo : lo + PIECE] for j in range(PER)]
        pieces.append(jnp.zeros((BS, 2 * LANES - USED), jnp.bfloat16))
        out_ref[e] = jnp.concatenate(pieces, axis=1)


def extra_rows(panel):
    devices = panel.shape[0] // PAGES
    return pl.pallas_call(
        extra_kernel,
        grid=(devices,),
        in_specs=[pl.BlockSpec((PAGES, BS, LANES), lambda i: (i, 0, 1))],
        out_specs=pl.BlockSpec((EXTRA, BS, 2 * LANES), lambda i: (i, 0, 0)),
        out_shape=jax.ShapeDtypeStruct((devices * EXTRA, BS, 2 * LANES), jnp.bfloat16),
    )(panel)


def product_kernel(
    base_ref, page_ref, target_ref, a0, a1, a2, a3, panel, extra, out_ref, pages, acc, sems
):
    step = pl.program_id(0)
    steps = pl.num_programs(0)
    n_panel = panel.shape[0]

    def fetch(at):
        slot = lax.rem(at, 2)
        first = (base_ref[0] + at) * SLOTS
        for g in range(SLOTS):
            page = page_ref[first + g]

            @pl.when(page < n_panel)
            def _():
                pltpu.make_async_copy(panel.at[page], pages.at[slot, g], sems.at[slot]).start()

            @pl.when(page >= n_panel)
            def _():
                pltpu.make_async_copy(
                    extra.at[page - n_panel], pages.at[slot, g], sems.at[slot]
                ).start()

    @pl.when(step == 0)
    def _():
        fetch(step)

    @pl.when(step + 1 < steps)
    def _():
        fetch(step + 1)

    acc[...] = jnp.zeros_like(acc)
    slot = lax.rem(step, 2)
    pltpu.make_async_copy(panel.at[pl.ds(0, SLOTS)], pages.at[slot], sems.at[slot]).wait()
    first = (base_ref[0] + step) * SLOTS
    for g in range(SLOTS):
        a = (a0, a1, a2, a3)[g // 4][0, g % 4]
        r = jnp.dot(a, pages[slot, g], preferred_element_type=jnp.float32)
        lo, hi = r[:, :LANES], r[:, LANES:]
        at = (first + g) * NZB
        u0, u1, u2 = target_ref[at], target_ref[at + 1], target_ref[at + 2]
        acc[0, u0] += lo
        acc[1, u1] += lo
        acc[2, u1] += hi
        acc[3, u2] += hi
    cut = LANES - BS
    for u in range(NZC):
        c0 = acc[0, u][:, :BS]
        c1 = jnp.concatenate([acc[1, u][:, BS:], acc[2, u][:, : BS - cut]], axis=1)
        c2 = acc[3, u][:, BS - cut : 2 * BS - cut]
        out_ref[0, u] = (c0 + c1 + c2).astype(out_ref.dtype)


def product(base, page, target, a_parts, panel, extra, rows):
    a_spec = pl.BlockSpec((1, 4, BS, BS), lambda i, base, page, target: (base[0] + i, 0, 0, 0))
    any_spec = pl.BlockSpec(memory_space=pl.ANY)
    grid_spec = pltpu.PrefetchScalarGridSpec(
        num_scalar_prefetch=3,
        grid=(rows,),
        in_specs=[a_spec] * 4 + [any_spec] * 2,
        out_specs=pl.BlockSpec((1, NZC, BS, BS), lambda i, *_: (i, 0, 0, 0)),
        scratch_shapes=[
            pltpu.VMEM((2, SLOTS, BS, 2 * LANES), jnp.bfloat16),
            pltpu.VMEM((4, NZC + 1, BS, LANES), jnp.float32),
            pltpu.SemaphoreType.DMA((2,)),
        ],
    )
    return pl.pallas_call(
        product_kernel,
        grid_spec=grid_spec,
        out_shape=jax.ShapeDtypeStruct((rows, NZC, BS, BS), jnp.bfloat16),
        compiler_params=pltpu.CompilerParams(vmem_limit_bytes=VMEM),
        cost_estimate=pl.CostEstimate(
            flops=2 * rows * SLOTS * BS * BS * 256,
            bytes_accessed=rows * SLOTS * BS * 512,
            transcendentals=0,
        ),
    )(base, page, target, *a_parts, panel, extra)


def around(axis, n, d):
    return functools.partial(lax.ppermute, axis_name=axis, perm=[(k, (k + d) % n) for k in range(n)])


def on_device(a_blocks, a_columns, b_blocks, b_order, b_columns, c_columns):
    rows = a_blocks.shape[0]
    n_col = lax.axis_size("col")
    panel = lax.all_gather(pack_b(b_blocks), "row", axis=0, tiled=True)

    a_parts, column_parts = [a_blocks], [a_columns]
    for d in range(1, n_col):
        a_parts.append(around("col", n_col, d)(a_blocks))
        column_parts.append(around("col", n_col, d)(a_columns))

    notes = jnp.concatenate([b_order, b_columns.reshape(-1)])[None]
    notes = lax.all_gather(notes, "row", axis=0, tiled=True)
    order = notes[:, :KBP].reshape(-1)
    columns_b = notes[:, KBP:].reshape(-1, NZB)
    wanted = jnp.concatenate(column_parts, axis=1).reshape(-1, 1)
    same = wanted == order[None, :]
    stored_ids = jnp.arange(order.shape[0], dtype=jnp.int32)
    stored = jnp.sum(jnp.where(same, stored_ids[None, :], 0), axis=1)
    device, row = stored // KBP, stored % KBP
    n_panel = panel.shape[0]
    page = jnp.where(row < PAGES, device * PAGES + row, n_panel + device * EXTRA + row - PAGES)
    targets = []
    for t in range(NZB):
        column = jnp.sum(jnp.where(same, columns_b[:, t][None, :], 0), axis=1).reshape(rows, SLOTS)
        match = column[:, :, None] == c_columns[:, None, :]
        slot_ids = jnp.arange(NZC, dtype=jnp.int32)
        slot = jnp.sum(jnp.where(match, slot_ids, 0), axis=2)
        targets.append(jnp.where(jnp.any(match, axis=2), slot, NZC))
    target = jnp.stack(targets, axis=2).reshape(-1).astype(jnp.int32)

    extra = extra_rows(panel)
    half = rows // 2
    me = lax.axis_index("layer").astype(jnp.int32)
    run = functools.partial(product, page=page, target=target, a_parts=a_parts, panel=panel, extra=extra, rows=half)
    sent = run(((1 - me) * half).reshape(1))
    got = lax.ppermute(sent, "layer", [(0, 1), (1, 0)])
    kept = run((me * half).reshape(1))
    return (kept.astype(jnp.float32) + got.astype(jnp.float32)).astype(jnp.bfloat16)


def solution(mesh):
    in_specs = (
        P("row", ("col", "layer"), None, None),
        P("row", ("col", "layer")),
        P(("row", "layer"), "col", None, None),
        P(("row", "layer")),
        P(("row", "layer"), "col"),
        P("row", "col"),
    )
    out_specs = P(("row", "layer"), "col", None, None)
    return jax.shard_map(
        on_device, mesh=mesh, in_specs=in_specs, out_specs=out_specs, check_vma=False
    )
```

time: 842 us -> 254 us (0.30)
  other arithmetic: 272 us -> 6.04 us
  waiting for transfers between devices: 300 us -> 36 us
  local copies, waits for them, and re-layouts: 139 us -> 4.29 us
  Pallas kernels: 0 us -> 61.2 us
  blocking collectives: 67.4 us -> 120 us
  matrix products: 43.4 us -> 0 us
  starting transfers between devices: 0.11 us -> 9.47 us
    scatter-add x16 -> x0, other arithmetic: 255 us -> none  [one_slot(): running.at[target.reshape(-1)]]
    all_gather x2 -> x1, waiting for transfers between devices: 282 us -> 36 us  [on_device(): panel = lax.all_gather(pack_b(b_blocks), 'row', axis=0, tiled=True)]
    unnamed x1, blocking collectives: 14.3 us -> 120 us
    gather x64 -> x0, local copies, waits for them, and re-layouts: 74.5 us -> none  [the longest x16 52.8 us: one_slot(): b_square = panel_blocks[stored]]
    pallas_call x0 -> x4, Pallas kernels: none -> 61.2 us  [the longest x2 39.3 us: product(): pl.pallas_call(product_kernel, grid_spec=grid_spec, out_shape=jax.ShapeDt...]
    all_gather x2 -> x0, blocking collectives: 53.1 us -> none  [the longest x1 43.8 us: on_device(): lax.all_gather(b_columns, 'row', axis=0, tiled=True)]
    reshape x16 -> x3, local copies, waits for them, and re-layouts: 47.9 us -> 0.45 us  [the longest x1 0.21 us: on_device(): target = jnp.stack(targets, axis=2).reshape(-1).astype(jnp.int32)]
    dot_general x16 -> x0, matrix products: 43.4 us -> none  [one_slot(): jnp.einsum('rab,rtbc->rtac', a_square, b_square, preferred_element_type=j...]
  transfers between devices with their start and end apart: 3 -> 8, of which waited for: 3 -> 1; matrix products, arithmetic and copies ran while one was open for 1% -> 2% of each run, Pallas kernels for 0% -> 16%
where the time goes in v1:
time: 254 us; the launch traced here: 251 us
  blocking collectives  120 us (47%)
  Pallas kernels  61.2 us (24%)
  waiting for transfers between devices  36 us (14%)
  between operations  14.3 us (6%)
  starting transfers between devices  9.47 us (4%)
  other arithmetic  6.04 us (2%)
  local copies, waits for them, and re-layouts  4.29 us (2%)
    unnamed x1, blocking collectives  120 us
    pallas_call x2, Pallas kernels, product(): pl.pallas_call(product_kernel, grid_spec=grid_spec, out_shape=jax.ShapeDt...  39.3 us
    all_gather x1, waiting for transfers between devices, on_device(): panel = lax.all_gather(pack_b(b_blocks), 'row', axis=0, tiled=True)  36 us
    pallas_call x1, Pallas kernels, extra_rows(): pl.pallas_call(extra_kernel, grid=(devices,), in_specs=[pl.BlockSpec((PAG...  20.7 us
    ppermute x3, starting transfers between devices, on_device(): column_parts.append(around('col', n_col, d)(a_columns))  6.51 us
    convert_element_type x1, other arithmetic, on_device(): (kept.astype(jnp.float32) + got.astype(jnp.float32)).astype(jnp.bfloat16)  5.09 us
  transfers between devices with their start and end apart: 8, of which 1 were waited for; matrix products, arithmetic and copies ran while one was open for 2% of the time, Pallas kernels for 16%

profile of v1, /device:TPU:1, one launch (start us, length us, event | category | flops | bytes accessed | tf_op | source)
XLA Modules:
  0.0 251.1 jit_solution(12234450980993948353)
XLA Ops:
  6.5 1.4 copy-done.1
  8.0 1.2 shard_map.64
  9.2 3.8 %collective-permute-start.1 = (s32[32,4]{0,1:T(4,128)S(1)}, s32[32,4]{0,1:T(4,128)S(1)}, u32[]{:S(2)}, u32[]{:S(2)}) collective-permute-start(s32[32,4]{0,1:T(4,128)S(1)} %copy-done.4), channel_id=1, source_target_pairs={{0,4},{2,6},{4,0},{6,2},{1,5},{3,7},{5,1},{7,3},{8,12},{10,14},{12... | collective-permute-start | bytes 1544 | tf_op jit(solution)/shard_map/ppermute | solution.py:160
  13.0 0.4 collective-permute-start
  13.4 2.3 collective-permute-start.2
  15.7 0.9 collective-permute-start.4
  16.7 0.1 copy.23
  16.9 0.7 dynamic-slice
  18.3 0.2 add_dynamic-update-slice_fusion
  18.5 119.9 %all-reduce = s32[2688]{0:T(1024)S(1)} all-reduce(s32[2688]{0:T(1024)S(1)} %add_dynamic-update-slice_fusion), channel_id=2, replica_groups=mesh['row'=32,'col'=4,'layer'=2] {'row'}, use_global_device_ids=true, to_apply=%add | all-reduce | flops 2688 | bytes 21504
  138.4 0.1 reshape.69
  138.5 0.2 reshape.66
  138.7 0.6 slice_reduce_fusion.2
  139.3 0.1 eq.62
  139.4 0.5 collective-permute-start.3
  140.1 0.6 fusion.1
  141.3 0.2 copy.27
  141.5 0.2 reshape.67.target_ref
  141.7 36.0 %all-gather.3.cloned.1.call-done.p_ref.panel = bf16[576,72,256]{2,1,0:T(8,128)(2,1)} async-done(((bf16[18,72,256]{2,1,0:T(8,128)(2,1)}), bf16[576,72,256]{2,1,0:T(8,128)(2,1)}) %all-gather.3.cloned.1.call-update) | async-done | bytes 21233680 | tf_op jit(solution)/shard_map/all_gather | solution.py:155
  177.7 20.7 %shard_map.65.extra = bf16[96,72,256]{2,1,0:T(8,128)(2,1)} custom-call(bf16[576,72,256]{2,1,0:T(8,128)(2,1)} %all-gather.3.cloned.1.call-done.p_ref.panel), custom_call_target="tpu_custom_call" | custom-call | tf_op jit(solution)/shard_map/pallas_call | solution.py:59
  198.4 19.7 %shard_map.67 = bf16[16,10,72,72]{3,2,1,0:T(8,128)(2,1)} custom-call(s32[1]{0:T(128)} %bitcast.5.base_ref, s32[512]{0:T(512)S(1)} %add_select_fusion.2.page_ref, s32[1536]{0:T(1024)S(1)} %reshape.67.target_ref, bf16[32,4,72,72]{3,2,1,0:T(8,128)(2,1)S(1)} %copy-done, bf16[32,4,72,72]{3,2,1,0:T(8,128)(2,1)} %collective-permute-done.3.a1, ...), custom_call_target="tpu_custom_call" | custom-call | flops 679477248 | bytes 9437184 | tf_op jit(solution)/shard_map/pallas_call | solution.py:135
  218.0 1.5 collective-permute-start.6
  219.5 19.7 %shard_map.66 = bf16[16,10,72,72]{3,2,1,0:T(8,128)(2,1)} custom-call(s32[1]{0:T(128)} %bitcast.base_ref, s32[512]{0:T(512)S(1)} %add_select_fusion.2.page_ref, s32[1536]{0:T(1024)S(1)} %reshape.67.target_ref, bf16[32,4,72,72]{3,2,1,0:T(8,128)(2,1)S(1)} %copy-done, bf16[32,4,72,72]{3,2,1,0:T(8,128)(2,1)} %collective-permute-done.3.a1, ...), custom_call_target="tpu_custom_call" | custom-call | flops 679477248 | bytes 9437184 | tf_op jit(solution)/shard_map/pallas_call | solution.py:135
  239.2 5.1 %add_convert_fusion = bf16[16,10,72,72]{3,2,1,0:T(8,128)(2,1)} fusion(bf16[16,10,72,72]{3,2,1,0:T(8,128)(2,1)} %collective-permute-done.6, bf16[16,10,72,72]{3,2,1,0:T(8,128)(2,1)} %shard_map.66), kind=kLoop, calls=%fused_computation | loop fusion | flops 3317760 | bytes 4976640 | tf_op jit(solution)/shard_map/convert_element_type | solution.py:189
  (41 shorter events, 1.0 us)
Async XLA Ops:
  6.5 10.3 %copy-start.6 = (u32[256]{0:T(256)S(1)}, u32[256]{0:T(256)}, u32[]{:S(2)}) copy-start(u32[256]{0:T(256)} %constant.48) | copy-start | bytes 3076
  6.5 9.2 %copy-start = (bf16[32,4,72,72]{3,2,1,0:T(8,128)(2,1)S(1)}, bf16[32,4,72,72]{3,2,1,0:T(8,128)(2,1)}, u32[]{:S(2)}) copy-start(bf16[32,4,72,72]{3,2,1,0:T(8,128)(2,1)} %a0.3) | copy-start | bytes 3981316
  6.5 171.1 %all-gather.3.cloned.1.call-start = ((), (), s32[]{:S(2)}) async-start(), calls=%async_computation | async-start | bytes 21897216 | tf_op jit(solution)/shard_map/all_gather | solution.py:155
  6.5 1.4 copy-start.1
  8.0 1.2 copy-start.4
  8.0 8.7 %copy-start.3 = (s32[21,3]{0,1:T(4,128)S(1)}, s32[21,3]{0,1:T(4,128)}, u32[]{:S(2)}) copy-start(s32[21,3]{0,1:T(4,128)} %param.10) | copy-start | bytes 760
  8.0 10.3 %copy-start.5 = (s32[21]{0:T(128)S(1)}, s32[21]{0:T(128)}, u32[]{:S(2)}) copy-start(s32[21]{0:T(128)} %param.9) | copy-start | bytes 256
  8.0 133.2 %copy-start.2 = (s32[32,10]{0,1:T(8,128)S(1)}, s32[32,10]{0,1:T(8,128)}, u32[]{:S(2)}) copy-start(s32[32,10]{0,1:T(8,128)} %param.11) | copy-start | bytes 3844
  9.2 130.2 %collective-permute-start.1 = (s32[32,4]{0,1:T(4,128)S(1)}, s32[32,4]{0,1:T(4,128)S(1)}, u32[]{:S(2)}, u32[]{:S(2)}) collective-permute-start(s32[32,4]{0,1:T(4,128)S(1)} %copy-done.4), channel_id=1, source_target_pairs={{0,4},{2,6},{4,0},{6,2},{1,5},{3,7},{5,1},{7,3},{8,12},{10,14},{12... | collective-permute-start | bytes 1544 | tf_op jit(solution)/shard_map/ppermute | solution.py:160
  13.0 126.9 %collective-permute-start = (s32[32,4]{0,1:T(4,128)S(1)}, s32[32,4]{0,1:T(4,128)S(1)}, u32[]{:S(2)}, u32[]{:S(2)}) collective-permute-start(s32[32,4]{0,1:T(4,128)S(1)} %copy-done.4), channel_id=1, source_target_pairs={{0,2},{2,4},{4,6},{6,0},{1,3},{3,5},{5,7},{7,1},{8,10},{10,12},{12... | collective-permute-start | bytes 1544 | tf_op jit(solution)/shard_map/ppermute | solution.py:160
  13.4 126.5 %collective-permute-start.2 = (s32[32,4]{0,1:T(4,128)S(1)}, s32[32,4]{0,1:T(4,128)S(1)}, u32[]{:S(2)}, u32[]{:S(2)}) collective-permute-start(s32[32,4]{0,1:T(4,128)S(1)} %copy-done.4), channel_id=1, source_target_pairs={{0,6},{2,0},{4,2},{6,4},{1,7},{3,1},{5,3},{7,5},{8,14},{10,8},{12,... | collective-permute-start | bytes 1544 | tf_op jit(solution)/shard_map/ppermute | solution.py:160
  15.7 182.6 %collective-permute-start.5 = (bf16[32,4,72,72]{3,2,1,0:T(8,128)(2,1)S(1)}, bf16[32,4,72,72]{3,2,1,0:T(8,128)(2,1)}, u32[]{:S(2)}, u32[]{:S(2)}) collective-permute-start(bf16[32,4,72,72]{3,2,1,0:T(8,128)(2,1)S(1)} %copy-done), channel_id=1, source_target_pairs={{0,6},{2,0},{4,2},{6,4},{1,7},{3,1},{5,3},{7,5},{8,14},{10,8},{12,... | collective-permute-start | bytes 3981320 | tf_op jit(solution)/shard_map/ppermute | solution.py:159
  15.7 182.6 %collective-permute-start.4 = (bf16[32,4,72,72]{3,2,1,0:T(8,128)(2,1)S(1)}, bf16[32,4,72,72]{3,2,1,0:T(8,128)(2,1)}, u32[]{:S(2)}, u32[]{:S(2)}) collective-permute-start(bf16[32,4,72,72]{3,2,1,0:T(8,128)(2,1)S(1)} %copy-done), channel_id=1, source_target_pairs={{0,4},{2,6},{4,0},{6,2},{1,5},{3,7},{5,1},{7,3},{8,12},{10,14},{12... | collective-permute-start | bytes 3981320 | tf_op jit(solution)/shard_map/ppermute | solution.py:159
  139.4 59.0 %collective-permute-start.3 = (bf16[32,4,72,72]{3,2,1,0:T(8,128)(2,1)S(1)}, bf16[32,4,72,72]{3,2,1,0:T(8,128)(2,1)}, u32[]{:S(2)}, u32[]{:S(2)}) collective-permute-start(bf16[32,4,72,72]{3,2,1,0:T(8,128)(2,1)S(1)} %copy-done), channel_id=1, source_target_pairs={{0,2},{2,4},{4,6},{6,0},{1,3},{3,5},{5,7},{7,1},{8,10},{10,12},{12... | collective-permute-start | bytes 3981320 | tf_op jit(solution)/shard_map/ppermute | solution.py:159
  218.0 21.1 %collective-permute-start.6 = (bf16[16,10,72,72]{3,2,1,0:T(8,128)(2,1)}, bf16[16,10,72,72]{3,2,1,0:T(8,128)(2,1)}, u32[]{:S(2)}, u32[]{:S(2)}) collective-permute-start(bf16[16,10,72,72]{3,2,1,0:T(8,128)(2,1)} %shard_map.67), channel_id=1, source_target_pairs={{0,1},{1,0},{2,3},{3,2},{4,5},{5,4},{6,7},{7,6},{8,9},{9,8},{10,11... | collective-permute-start | bytes 4976648 | tf_op jit(solution)/shard_map/ppermute | solution.py:187
Sparse Core Ops, SparseCore 0:
  9.9 167.6 all-gather.2

commit v2 on v1

--- a/solution.py
+++ b/solution.py
@@ -18,6 +18,7 @@
 PIECE = NZB * BS // PER
 USED = NZB * BS
 SLOTS = 16
+TOGETHER = 4
 VMEM = 48 * 1024 * 1024
 
 
@@ -48,20 +49,22 @@
 
 def extra_kernel(p_ref, out_ref):
     lo = USED - LANES
-    for e in range(EXTRA):
-        pieces = [p_ref[e * PER + j][:, lo : lo + PIECE] for j in range(PER)]
-        pieces.append(jnp.zeros((BS, 2 * LANES - USED), jnp.bfloat16))
-        out_ref[e] = jnp.concatenate(pieces, axis=1)
+    for e in range(out_ref.shape[0]):
+        for t in range(NZB):
+            two = [p_ref[e * PER + 2 * t + j][:, lo : lo + PIECE] for j in range(2)]
+            out_ref[e, :, t * BS : (t + 1) * BS] = jnp.concatenate(two, axis=1)
+        out_ref[e, :, USED:] = jnp.zeros((BS, 2 * LANES - USED), jnp.bfloat16)
 
 
 def extra_rows(panel):
     devices = panel.shape[0] // PAGES
     return pl.pallas_call(
         extra_kernel,
-        grid=(devices,),
-        in_specs=[pl.BlockSpec((PAGES, BS, LANES), lambda i: (i, 0, 1))],
-        out_specs=pl.BlockSpec((EXTRA, BS, 2 * LANES), lambda i: (i, 0, 0)),
+        grid=(devices // TOGETHER,),
+        in_specs=[pl.BlockSpec((TOGETHER * PAGES, BS, LANES), lambda i: (i, 0, 1))],
+        out_specs=pl.BlockSpec((TOGETHER * EXTRA, BS, 2 * LANES), lambda i: (i, 0, 0)),
         out_shape=jax.ShapeDtypeStruct((devices * EXTRA, BS, 2 * LANES), jnp.bfloat16),
+        compiler_params=pltpu.CompilerParams(vmem_limit_bytes=VMEM),
     )(panel)
 
 

time: 254 us -> 253 us (level)
  Pallas kernels: 61.2 us -> 57.2 us
    pallas_call x1, Pallas kernels: 20.7 us -> 16.7 us  [extra_rows(): pl.pallas_call(extra_kernel, grid=(devices // TOGETHER,), in_specs=[pl.Bl...]
  transfers between devices with their start and end apart: 8 -> 8, of which waited for: 1 -> 1; matrix products, arithmetic and copies ran while one was open for 2% -> 2% of each run, Pallas kernels for 16% -> 14%
where the time goes in v2:
time: 253 us; the launch traced here: 251 us
  blocking collectives  120 us (47%)
  Pallas kernels  57.2 us (23%)
  waiting for transfers between devices  36 us (14%)
  between operations  14.3 us (6%)
  starting transfers between devices  11.6 us (5%)
  local copies, waits for them, and re-layouts  6.04 us (2%)
  other arithmetic  6.04 us (2%)
    unnamed x1, blocking collectives  120 us
    pallas_call x2, Pallas kernels, product(): pl.pallas_call(product_kernel, grid_spec=grid_spec, out_shape=jax.ShapeDt...  39.3 us
    all_gather x1, waiting for transfers between devices, on_device(): panel = lax.all_gather(pack_b(b_blocks), 'row', axis=0, tiled=True)  36 us
    pallas_call x1, Pallas kernels, extra_rows(): pl.pallas_call(extra_kernel, grid=(devices // TOGETHER,), in_specs=[pl.Bl...  16.7 us
    ppermute x3, starting transfers between devices, on_device(): column_parts.append(around('col', n_col, d)(a_columns))  6.51 us
    convert_element_type x1, other arithmetic, on_device(): (kept.astype(jnp.float32) + got.astype(jnp.float32)).astype(jnp.bfloat16)  5.09 us
  transfers between devices with their start and end apart: 8, of which 1 were waited for; matrix products, arithmetic and copies ran while one was open for 2% of the time, Pallas kernels for 14%

profile of v2, /device:TPU:1, one launch (start us, length us, event | category | flops | bytes accessed | tf_op | source)
XLA Modules:
  0.0 251.1 jit_solution(12972139790707636134)
XLA Ops:
  6.5 1.4 copy-done.2
  8.0 1.2 shard_map.64
  9.2 3.8 %collective-permute-start.1 = (s32[32,4]{0,1:T(4,128)S(1)}, s32[32,4]{0,1:T(4,128)S(1)}, u32[]{:S(2)}, u32[]{:S(2)}) collective-permute-start(s32[32,4]{0,1:T(4,128)S(1)} %copy-done.5), channel_id=1, source_target_pairs={{0,4},{2,6},{4,0},{6,2},{1,5},{3,7},{5,1},{7,3},{8,12},{10,14},{12... | collective-permute-start | bytes 1544 | tf_op jit(solution)/shard_map/ppermute | solution.py:163
  13.0 0.4 collective-permute-start
  13.4 2.3 collective-permute-start.2
  15.7 0.9 collective-permute-start.4
  16.9 0.7 dynamic-slice
  18.3 0.2 add_dynamic-update-slice_fusion
  18.5 119.9 %all-reduce = s32[2688]{0:T(1024)S(1)} all-reduce(s32[2688]{0:T(1024)S(1)} %add_dynamic-update-slice_fusion), channel_id=2, replica_groups=mesh['row'=32,'col'=4,'layer'=2] {'row'}, use_global_device_ids=true, to_apply=%add | all-reduce | flops 2688 | bytes 21504
  138.4 0.1 reshape.69
  138.5 0.2 reshape.66
  138.7 0.6 slice_reduce_fusion.2
  139.3 0.1 eq.62
  139.4 0.5 collective-permute-start.3
  140.1 0.6 fusion.1
  141.3 0.2 copy.27
  141.5 0.2 reshape.67.target_ref
  141.7 36.0 %all-gather.3.cloned.1.call-done.p_ref.panel = bf16[576,72,256]{2,1,0:T(8,128)(2,1)} async-done(((bf16[18,72,256]{2,1,0:T(8,128)(2,1)}), bf16[576,72,256]{2,1,0:T(8,128)(2,1)}) %all-gather.3.cloned.1.call-update) | async-done | bytes 21233680 | tf_op jit(solution)/shard_map/all_gather | solution.py:158
  177.7 16.7 %shard_map.65.extra = bf16[96,72,256]{2,1,0:T(8,128)(2,1)S(1)} custom-call(bf16[576,72,256]{2,1,0:T(8,128)(2,1)} %all-gather.3.cloned.1.call-done.p_ref.panel), custom_call_target="tpu_custom_call" | custom-call | tf_op jit(solution)/shard_map/pallas_call | solution.py:61
  194.4 1.7 copy-done
  196.2 19.6 %shard_map.67 = bf16[16,10,72,72]{3,2,1,0:T(8,128)(2,1)} custom-call(s32[1]{0:T(128)} %bitcast.5.base_ref, s32[512]{0:T(512)S(1)} %add_select_fusion.2.page_ref, s32[1536]{0:T(1024)S(1)} %reshape.67.target_ref, bf16[32,4,72,72]{3,2,1,0:T(8,128)(2,1)S(1)} %copy-done.1, bf16[32,4,72,72]{3,2,1,0:T(8,128)(2,1)} %collective-permute-done.3.a1, ...), custom_call_target="tpu_custom_call" | custom-call | flops 679477248 | bytes 9437184 | tf_op jit(solution)/shard_map/pallas_call | solution.py:138
  215.9 3.6 %collective-permute-start.6 = (bf16[16,10,72,72]{3,2,1,0:T(8,128)(2,1)}, bf16[16,10,72,72]{3,2,1,0:T(8,128)(2,1)}, u32[]{:S(2)}, u32[]{:S(2)}) collective-permute-start(bf16[16,10,72,72]{3,2,1,0:T(8,128)(2,1)} %shard_map.67), channel_id=1, source_target_pairs={{0,1},{1,0},{2,3},{3,2},{4,5},{5,4},{6,7},{7,6},{8,9},{9,8},{10,11... | collective-permute-start | bytes 4976648 | tf_op jit(solution)/shard_map/ppermute | solution.py:190
  219.5 19.6 %shard_map.66 = bf16[16,10,72,72]{3,2,1,0:T(8,128)(2,1)} custom-call(s32[1]{0:T(128)} %bitcast.base_ref, s32[512]{0:T(512)S(1)} %add_select_fusion.2.page_ref, s32[1536]{0:T(1024)S(1)} %reshape.67.target_ref, bf16[32,4,72,72]{3,2,1,0:T(8,128)(2,1)S(1)} %copy-done.1, bf16[32,4,72,72]{3,2,1,0:T(8,128)(2,1)} %collective-permute-done.3.a1, ...), custom_call_target="tpu_custom_call" | custom-call | flops 679477248 | bytes 9437184 | tf_op jit(solution)/shard_map/pallas_call | solution.py:138
  239.2 5.1 %add_convert_fusion = bf16[16,10,72,72]{3,2,1,0:T(8,128)(2,1)} fusion(bf16[16,10,72,72]{3,2,1,0:T(8,128)(2,1)} %collective-permute-done.6, bf16[16,10,72,72]{3,2,1,0:T(8,128)(2,1)} %shard_map.66), kind=kLoop, calls=%fused_computation | loop fusion | flops 3317760 | bytes 4976640 | tf_op jit(solution)/shard_map/convert_element_type | solution.py:192
  (43 shorter events, 1.1 us)
Async XLA Ops:
  6.5 10.3 %copy-start.7 = (u32[256]{0:T(256)S(1)}, u32[256]{0:T(256)}, u32[]{:S(2)}) copy-start(u32[256]{0:T(256)} %constant.48) | copy-start | bytes 3076
  6.5 9.2 %copy-start.1 = (bf16[32,4,72,72]{3,2,1,0:T(8,128)(2,1)S(1)}, bf16[32,4,72,72]{3,2,1,0:T(8,128)(2,1)}, u32[]{:S(2)}) copy-start(bf16[32,4,72,72]{3,2,1,0:T(8,128)(2,1)} %a0.3) | copy-start | bytes 3981316
  6.5 171.1 %all-gather.3.cloned.1.call-start = ((), (), s32[]{:S(2)}) async-start(), calls=%async_computation | async-start | bytes 21897216 | tf_op jit(solution)/shard_map/all_gather | solution.py:158
  6.5 1.4 copy-start.2
  8.0 1.2 copy-start.5
  8.0 8.7 %copy-start.4 = (s32[21,3]{0,1:T(4,128)S(1)}, s32[21,3]{0,1:T(4,128)}, u32[]{:S(2)}) copy-start(s32[21,3]{0,1:T(4,128)} %param.10) | copy-start | bytes 760
  8.0 10.3 %copy-start.6 = (s32[21]{0:T(128)S(1)}, s32[21]{0:T(128)}, u32[]{:S(2)}) copy-start(s32[21]{0:T(128)} %param.9) | copy-start | bytes 256
  8.0 133.2 %copy-start.3 = (s32[32,10]{0,1:T(8,128)S(1)}, s32[32,10]{0,1:T(8,128)}, u32[]{:S(2)}) copy-start(s32[32,10]{0,1:T(8,128)} %param.11) | copy-start | bytes 3844
  9.2 130.2 %collective-permute-start.1 = (s32[32,4]{0,1:T(4,128)S(1)}, s32[32,4]{0,1:T(4,128)S(1)}, u32[]{:S(2)}, u32[]{:S(2)}) collective-permute-start(s32[32,4]{0,1:T(4,128)S(1)} %copy-done.5), channel_id=1, source_target_pairs={{0,4},{2,6},{4,0},{6,2},{1,5},{3,7},{5,1},{7,3},{8,12},{10,14},{12... | collective-permute-start | bytes 1544 | tf_op jit(solution)/shard_map/ppermute | solution.py:163
  13.0 126.9 %collective-permute-start = (s32[32,4]{0,1:T(4,128)S(1)}, s32[32,4]{0,1:T(4,128)S(1)}, u32[]{:S(2)}, u32[]{:S(2)}) collective-permute-start(s32[32,4]{0,1:T(4,128)S(1)} %copy-done.5), channel_id=1, source_target_pairs={{0,2},{2,4},{4,6},{6,0},{1,3},{3,5},{5,7},{7,1},{8,10},{10,12},{12... | collective-permute-start | bytes 1544 | tf_op jit(solution)/shard_map/ppermute | solution.py:163
  13.4 126.5 %collective-permute-start.2 = (s32[32,4]{0,1:T(4,128)S(1)}, s32[32,4]{0,1:T(4,128)S(1)}, u32[]{:S(2)}, u32[]{:S(2)}) collective-permute-start(s32[32,4]{0,1:T(4,128)S(1)} %copy-done.5), channel_id=1, source_target_pairs={{0,6},{2,0},{4,2},{6,4},{1,7},{3,1},{5,3},{7,5},{8,14},{10,8},{12,... | collective-permute-start | bytes 1544 | tf_op jit(solution)/shard_map/ppermute | solution.py:163
  15.7 180.5 %collective-permute-start.5 = (bf16[32,4,72,72]{3,2,1,0:T(8,128)(2,1)S(1)}, bf16[32,4,72,72]{3,2,1,0:T(8,128)(2,1)}, u32[]{:S(2)}, u32[]{:S(2)}) collective-permute-start(bf16[32,4,72,72]{3,2,1,0:T(8,128)(2,1)S(1)} %copy-done.1), channel_id=1, source_target_pairs={{0,6},{2,0},{4,2},{6,4},{1,7},{3,1},{5,3},{7,5},{8,14},{10,8},{12,... | collective-permute-start | bytes 3981320 | tf_op jit(solution)/shard_map/ppermute | solution.py:162
  15.7 180.5 %collective-permute-start.4 = (bf16[32,4,72,72]{3,2,1,0:T(8,128)(2,1)S(1)}, bf16[32,4,72,72]{3,2,1,0:T(8,128)(2,1)}, u32[]{:S(2)}, u32[]{:S(2)}) collective-permute-start(bf16[32,4,72,72]{3,2,1,0:T(8,128)(2,1)S(1)} %copy-done.1), channel_id=1, source_target_pairs={{0,4},{2,6},{4,0},{6,2},{1,5},{3,7},{5,1},{7,3},{8,12},{10,14},{12... | collective-permute-start | bytes 3981320 | tf_op jit(solution)/shard_map/ppermute | solution.py:162
  139.4 56.8 %collective-permute-start.3 = (bf16[32,4,72,72]{3,2,1,0:T(8,128)(2,1)S(1)}, bf16[32,4,72,72]{3,2,1,0:T(8,128)(2,1)}, u32[]{:S(2)}, u32[]{:S(2)}) collective-permute-start(bf16[32,4,72,72]{3,2,1,0:T(8,128)(2,1)S(1)} %copy-done.1), channel_id=1, source_target_pairs={{0,2},{2,4},{4,6},{6,0},{1,3},{3,5},{5,7},{7,1},{8,10},{10,12},{12... | collective-permute-start | bytes 3981320 | tf_op jit(solution)/shard_map/ppermute | solution.py:162
  194.4 1.8 copy-start
  215.9 23.3 %collective-permute-start.6 = (bf16[16,10,72,72]{3,2,1,0:T(8,128)(2,1)}, bf16[16,10,72,72]{3,2,1,0:T(8,128)(2,1)}, u32[]{:S(2)}, u32[]{:S(2)}) collective-permute-start(bf16[16,10,72,72]{3,2,1,0:T(8,128)(2,1)} %shard_map.67), channel_id=1, source_target_pairs={{0,1},{1,0},{2,3},{3,2},{4,5},{5,4},{6,7},{7,6},{8,9},{9,8},{10,11... | collective-permute-start | bytes 4976648 | tf_op jit(solution)/shard_map/ppermute | solution.py:190
Sparse Core Ops, SparseCore 0:
  9.9 167.6 all-gather.2
